TPU v7x, 128 devices: a whole 4x4x4 slice. The times are simulated.
128 devices in a mesh: seq: 16 (over x, y), head: 8 (over z, core).
Axes of the slice: x: 4, y: 4, z: 4, core: 2. Of those that a mesh axis runs over, the one named last changes fastest.
Arguments:
- hidden: bfloat16 [2, 4096, 2048], P(None, 'seq', 'head'), may hold values from -6 to 6
- cotangent: float32 [2, 4096, 2048], P(None, 'seq', 'head'), may hold values from -6 to 6
- opening_flags: int32 [2, 4096], P(None, 'seq'), may hold values from 0 to 1, as said below
- vectors: bfloat16 [1, 16, 2048], P(None, 'seq', 'head'), may hold values from -9 to 2, as said below
- shift_first: bfloat16 [1, 160, 2048], P(None, 'seq', 'head'), may hold values from -0.125 to 0.125
- shift_second: bfloat16 [1, 160, 2048], P(None, 'seq', 'head'), may hold values from -1 to 1
- decay_first: bfloat16 [1, 64, 2048], P(None, 'seq', 'head'), may hold values from -0.125 to 0.125
- decay_second: bfloat16 [1, 64, 2048], P(None, 'seq', 'head'), may hold values from -0.75 to 0.75
- time_weights: bfloat16 [1, 4, 2048, 2048], P(None, None, 'seq', 'head'), may hold values from -0.125 to 0.125
- time_output: bfloat16 [1, 2048, 2048], P(None, 'head', 'seq'), may hold values from -0.125 to 0.125
- channel_key: bfloat16 [1, 2048, 7168], P(None, 'seq', 'head'), may hold values from -0.125 to 0.125
- channel_value: bfloat16 [1, 7168, 2048], P(None, 'head', 'seq'), may hold values from -0.0625 to 0.0625
- channel_recept: bfloat16 [1, 2048, 2048], P(None, 'seq', 'head'), may hold values from -0.125 to 0.125
Outputs:
- result: float32 [2, 4096, 2048], P(None, 'seq', 'head')
- hidden_grad: float32 [2, 4096, 2048], P(None, 'seq', 'head')
- vectors_grad: float32 [1, 16, 2048], P(None, 'seq', 'head')
- shift_first_grad: float32 [1, 160, 2048], P(None, 'seq', 'head')
- shift_second_grad: float32 [1, 160, 2048], P(None, 'seq', 'head')
- decay_first_grad: float32 [1, 64, 2048], P(None, 'seq', 'head')
- decay_second_grad: float32 [1, 64, 2048], P(None, 'seq', 'head')
- time_weights_grad: float32 [1, 4, 2048, 2048], P(None, None, 'seq', 'head')
- time_output_grad: float32 [1, 2048, 2048], P(None, 'head', 'seq')
- channel_key_grad: float32 [1, 2048, 7168], P(None, 'seq', 'head')
- channel_value_grad: float32 [1, 7168, 2048], P(None, 'head', 'seq')
- channel_recept_grad: float32 [1, 2048, 2048], P(None, 'seq', 'head')
Inputs may be any that keep to these rules, and one draw needn't show every extreme that they name: `opening_flags`: 1 marks the first token of a sequence, where token shift and WKV state restart; position 0 of every batch row is 1; one batch row, drawn from the seed, holds a single sequence, the others up to four. `vectors`: row 8 lies in -9 to -3; rows 2 to 7, 14 and 15 in 0 to 2.
All inputs are finite; a program needn't handle non-finite values.
Results may differ from a plain program's by a relative error of at most 0.03.
Values may be sent and summed in bfloat16 or wider, within the bound.
A program may use at most 192 MiB of HBM per device.

v0:
```python
import functools
from types import SimpleNamespace

import jax
import jax.numpy as jnp
import numpy as np
from jax import lax
from jax.experimental import pallas as pl
from jax.experimental.pallas import tpu as pltpu
from jax.sharding import PartitionSpec as P

MESH = pl.DeviceIdType.MESH
BF = jnp.bfloat16
F32 = jnp.float32
EPS = 1e-5
GEPS = 64e-5
N = 512
TB = 256
TC = 32
W = 256
C = 64
LV = 6
D = 2048
FFL = 896
VMEM_LIMIT = 63 * 2**20
R_FIRST, R_SECOND, R_DECAY1, R_VEC, R_DECAY2 = 0, 160, 320, 384, 400


def nt(a, b):
    return lax.dot_general(a, b, (((1,), (1,)), ((), ())), preferred_element_type=F32)


def nn(a, b):
    return jnp.dot(a, b, preferred_element_type=F32)


def place():
    return lax.axis_index("seq"), lax.axis_index("head")


def sibling():
    s, h = place()
    return s, h // 2 * 2 + 1 - lax.rem(h, 2)


def chip(k, core=0):
    h = place()[1]
    c = lax.rem(h, 2)
    return lax.rem(h // 2 + k, 4) * 2 + (1 - c if core else c)


def zdev(k):
    return place()[0], chip(k)


def seq_index(first, ka, kb):
    s = place()[0]
    x, y = s // 4, lax.rem(s, 4)
    if first:
        return lax.rem(x + ka, 4) * 4 + lax.rem(y + kb, 4)
    return lax.rem(x + kb, 4) * 4 + lax.rem(y + ka, 4)


def seq_dev(first, ka, kb):
    return seq_index(first, ka, kb), place()[1]


class Copy:
    def __init__(self, net, i, make):
        self.net, self.i, self.make = net, i, make

    def desc(self):
        src, dst, dev = self.make()
        return pltpu.make_async_remote_copy(
            src_ref=src,
            dst_ref=dst,
            send_sem=self.net.ss.at[self.i],
            recv_sem=self.net.rs.at[self.i],
            device_id=dev,
            device_id_type=MESH,
        )

    def start(self):
        self.desc().start()
        self.net.out.append(self)

    def wait_recv(self):
        self.desc().wait_recv()

    def wait_send(self):
        self.desc().wait_send()


class Net:
    def __init__(self, ss, rs):
        self.ss, self.rs, self.n, self.out = ss, rs, 0, []

    def copy(self, make):
        self.n += 1
        return Copy(self, self.n - 1, make)

    def drain(self, copies=None):
        for c in list(self.out) if copies is None else copies:
            c.wait_send()
            self.out.remove(c)


def greet(peers):
    b = pltpu.get_barrier_semaphore()
    for p in peers:
        pl.semaphore_signal(b, inc=1, device_id=p, device_id_type=MESH)
    pl.semaphore_wait(b, len(peers))


def head_peers():
    s, h = place()
    return [(s, lax.rem(h + k, 8)) for k in range(1, 8)]


def seq_peers():
    s, h = place()
    return [(lax.rem(s + k, 16), h) for k in range(1, 16)]


def diagonal_peers(step):
    s, h = place()
    return [(lax.rem(s + step, 16), lax.rem(h + k, 8)) for k in range(1, 8)]


ORDER = (1, 3, 2)


def half(ref, i):
    n = ref.shape[0]
    m = n // 2 if len(ref.shape) == 3 else (n // 2 + 15) // 16 * 16
    return ref.at[m:n] if i else ref.at[0:m]


class HeadGather:
    def __init__(self, net, slot):
        self.net = net

        def own():
            return slot(place()[1])

        def at(k):
            return slot(chip(k))

        def copy(ref, dev):
            return net.copy(lambda: (ref(), ref(), dev()))

        up, down = lambda: zdev(1), lambda: zdev(3)
        self.ua = copy(lambda: half(own(), 0), up)
        self.db = copy(lambda: half(own(), 1), down)
        self.ub = copy(lambda: half(own(), 1), up)
        self.da = copy(lambda: half(own(), 0), down)
        self.mine = copy(own, sibling)
        self.fa = copy(lambda: half(at(3), 0), up)
        self.fb = copy(lambda: half(at(1), 1), down)
        self.s3 = copy(lambda: at(3), sibling)
        self.s1 = copy(lambda: at(1), sibling)
        self.sa = copy(lambda: half(at(2), 0), sibling)
        self.sb = copy(lambda: half(at(2), 1), sibling)

    def start(self):
        for c in (self.ua, self.db, self.ub, self.da, self.mine):
            c.start()

    def relay(self):
        self.ua.wait_recv()
        self.fa.start()
        self.db.wait_recv()
        self.fb.start()
        self.ub.wait_recv()
        self.s3.start()
        self.da.wait_recv()
        self.s1.start()

    def relay_far(self):
        self.fa.wait_recv()
        self.sa.start()
        self.fb.wait_recv()
        self.sb.start()

    def finish(self):
        for c in (self.mine, self.s3, self.s1, self.sa, self.sb):
            c.wait_recv()

    def drain(self):
        near = [self.ua, self.db, self.ub, self.da, self.mine]
        self.net.drain(near + [self.fa, self.fb, self.s3, self.s1, self.sa, self.sb])


class HeadScatter:
    def __init__(self, net, part, fromsib, tosend, fromz):
        self.net, self.part, self.fromsib, self.tosend, self.fromz = net, part, fromsib, tosend, fromz
        self.a = {
            k: net.copy(lambda k=k: (part.at[chip(k, 1)], fromsib.at[k], sibling()))
            for k in range(4)
        }

        def copy(i, j, k, dev):
            return net.copy(lambda: (half(tosend.at[i], k), half(fromz.at[j], k), zdev(dev)))

        self.fa, self.fb = copy(1, 2, 0, 1), copy(1, 2, 1, 3)
        self.ua, self.ub = copy(0, 0, 0, 1), copy(0, 0, 1, 1)
        self.da, self.db = copy(2, 1, 0, 3), copy(2, 1, 1, 3)
        self.all = [*self.a.values(), self.fa, self.fb, self.ua, self.ub, self.da, self.db]

    def theirs(self, k):
        return chip(k, 1)

    def ours(self, k):
        return chip(k)

    def give(self, k):
        self.a[k].start()

    def both(self, k, i):
        own = half(self.part.at[chip(k)], i)[...].astype(F32)
        return own + half(self.fromsib.at[k], i)[...].astype(F32)

    def put(self, i, k, x):
        half(self.tosend.at[i], k)[...] = x.astype(BF)

    def pass_far(self):
        self.a[2].wait_recv()
        self.put(1, 0, self.both(2, 0))
        self.fa.start()
        self.put(1, 1, self.both(2, 1))
        self.fb.start()
        self.a[1].wait_recv()
        self.put(0, 1, self.both(1, 1))
        self.ub.start()
        self.a[3].wait_recv()
        self.put(2, 0, self.both(3, 0))
        self.da.start()

    def pass_near(self):
        far = self.fromz.at[2]
        self.fa.wait_recv()
        self.put(0, 0, self.both(1, 0) + half(far, 0)[...].astype(F32))
        self.ua.start()
        self.fb.wait_recv()
        self.put(2, 1, self.both(3, 1) + half(far, 1)[...].astype(F32))
        self.db.start()

    def total(self):
        self.a[0].wait_recv()
        t = self.part[chip(0)].astype(F32) + self.fromsib[0].astype(F32)
        for c in (self.ub, self.da, self.ua, self.db):
            c.wait_recv()
        return t + self.fromz[0].astype(F32) + self.fromz[1].astype(F32)

    def drain(self):
        self.net.drain(self.all)


class SeqGather:
    def __init__(self, net, src, slot, xfirst, sem):
        self.net, self.src, self.slot, self.sem = net, src, slot, sem

        def at(k):
            return slot(seq_index(xfirst, k, 0))

        self.first = {
            k: net.copy(lambda k=k: (src, at(0), seq_dev(xfirst, k, 0))) for k in ORDER
        }
        self.own2 = [
            net.copy(lambda k=k: (src, at(0), seq_dev(xfirst, 0, k))) for k in (1, 3)
        ]
        self.second = {
            (k, j): net.copy(lambda k=k, j=j: (at(4 - k), at(4 - k), seq_dev(xfirst, 0, j)))
            for k in ORDER
            for j in (1, 3)
        }

        def came(k, j):
            return slot(seq_index(xfirst, (4 - k) % 4, j))

        self.far = {
            k: net.copy(
                lambda k=k, j=j: (came(k, 4 - j), came(k, 4 - j), seq_dev(xfirst, 0, j))
            )
            for k, j in ((0, 1), (1, 1), (3, 3), (2, 3))
        }

    def local(self):
        return pltpu.make_async_copy(self.src, self.slot(place()[0]), self.sem)

    def p0(self):
        self.local().start()
        for c in self.first.values():
            c.start()

    def p1(self):
        self.p0()
        for c in self.own2:
            c.start()

    def p2(self, own=False):
        if own:
            for c in self.own2:
                c.start()
        for k in ORDER:
            self.first[k].wait_recv()
            for j in (1, 3):
                self.second[k, j].start()

    def p3(self):
        self.own2[0].wait_recv()
        self.far[0].start()
        for k, j in ((1, 1), (3, 3), (2, 3)):
            self.second[k, j].wait_recv()
            self.far[k].start()

    def finish(self):
        self.local().wait()
        self.own2[1].wait_recv()
        for k, j in ((1, 3), (3, 1), (2, 1)):
            self.second[k, j].wait_recv()
        for c in self.far.values():
            c.wait_recv()

    def drain(self):
        self.net.drain(
            [*self.first.values(), *self.own2, *self.second.values(), *self.far.values()]
        )


class SeqScatter:
    def __init__(self, net, src, recv, acc, recv2, xfirst, own_sem=None, sems=None):
        self.net, self.src, self.recv, self.acc, self.recv2 = net, src, recv, acc, recv2
        self.xfirst, self.own_sem, self.sems = xfirst, own_sem, sems
        f = xfirst
        self.c1 = {
            k: net.copy(
                lambda k=k: (src.at[pl.ds(self.line(0, k) * 4, 4)], recv.at[k - 1], seq_dev(f, k, 0))
            )
            for k in ORDER
        }
        self.c2 = {
            k: net.copy(lambda k=k: (acc.at[self.line(1, k)], recv2.at[k - 1], seq_dev(f, 0, k)))
            for k in ORDER
        }

    def line(self, axis, k):
        s = place()[0]
        x, y = s // 4, lax.rem(s, 4)
        return lax.rem((x if (axis == 0) == self.xfirst else y) + k, 4)

    def own(self):
        return pltpu.make_async_copy(
            self.src.at[pl.ds(self.line(0, 0) * 4, 4)], self.acc, self.own_sem
        )

    def near(self):
        self.c1[1].start()
        self.c1[3].start()

    def far(self):
        self.c1[2].start()

    def p2(self, stage=None):
        for k in ORDER:
            self.c1[k].wait_recv()
        if stage is None:
            a = self.line(0, 0) * 4

            def body(j):
                t = self.src[a + j].astype(F32) + self.recv[0, j].astype(F32)
                t = t + self.recv[1, j].astype(F32) + self.recv[2, j].astype(F32)
                self.acc[j] = t.astype(BF)

            fori(4, body)
        else:
            copies = [
                pltpu.make_async_copy(self.recv.at[:, j], stage[j % 2], self.sems.at[j])
                for j in range(4)
            ]
            copies[0].start()
            self.own().wait()
            for j in range(4):
                if j < 3:
                    copies[j + 1].start()
                copies[j].wait()
                st = stage[j % 2]
                t = self.acc[j].astype(F32) + st[0].astype(F32)
                self.acc[j] = (t + st[1].astype(F32) + st[2].astype(F32)).astype(BF)
        for k in ORDER:
            self.c2[k].start()

    def finish(self, out):
        for k in ORDER:
            self.c2[k].wait_recv()
        t = self.acc[self.line(1, 0)].astype(F32) + self.recv2[0].astype(F32)
        out[...] = t + self.recv2[1].astype(F32) + self.recv2[2].astype(F32)


def fori(n, body):
    def step(i, carry):
        body(i)
        return carry

    lax.fori_loop(0, n, step, 0)


def row_stats(x3):
    m = jnp.sum(jnp.sum(x3, axis=0), axis=1, keepdims=True) / D
    d = x3 - m[None]
    v = jnp.sum(jnp.sum(d * d, axis=0), axis=1, keepdims=True) / D
    return m, lax.rsqrt(v + EPS)


def iota(shape, dim):
    return lax.broadcasted_iota(jnp.int32, shape, dim)


def shift_down(u, first, keep):
    r = pltpu.roll(u, 1, 0)
    return jnp.where(iota(u.shape, 0) == 0, first, r) * keep


def shift_up(u):
    return jnp.where(iota(u.shape, 0) == u.shape[0] - 1, 0.0, pltpu.roll(u, u.shape[0] - 1, 0))


def rows_of(b):
    return slice(b * TB, (b + 1) * TB)


def slab_of(ref, i):
    return ref[:, i].reshape(TB, W)


class Norm1:
    def __init__(self, R):
        self.R = R

    def stats(self, b):
        R = self.R

        def body(i):
            at = pl.multiple_of(i * 64, 64)
            m, r = row_stats(R.xF[b, :, pl.ds(at, 64), :].astype(F32))
            R.mean[pl.ds(b * TB + at, 64), :] = m
            R.rstd[pl.ds(b * TB + at, 64), :] = r

        fori(4, body)

    def edge_stats(self):
        m, r = row_stats(self.R.bord[...].astype(F32))
        self.R.bmean[...] = m
        self.R.brstd[...] = r

    def block(self, i, b):
        R = self.R
        v = R.smF[i, R_VEC : R_VEC + 16, :].astype(F32)
        rows = rows_of(b)
        n = (R.xF[b, i].astype(F32) - R.mean[rows, :]) * R.rstd[rows, :]
        normed = n * v[0:1] + v[1:2]
        at = slice(16 * b, 16 * b + 16)
        e = (R.bord[i, at, :].astype(F32) - R.bmean[at, :]) * R.brstd[at, :]
        first = (e * v[0:1] + v[1:2])[15:16]
        differ = shift_down(normed, first, R.keep[rows, :]) - normed
        return n, normed, differ, v


def tree(r, k, wk, keep):
    row = iota((C, W), 0)
    p = jnp.broadcast_to(keep, (C, W))
    q = jnp.ones((C, W), F32)
    t = wk
    out = []
    for level in range(LV):
        m = 1 << level
        second = (row // m) % 2 == 1
        e = jnp.where(second, p, q)
        out.append((jnp.where(second, r, k), e))
        other = jnp.where(second, pltpu.roll(t, m, 0), pltpu.roll(t, C - m, 0))
        p = jnp.where(second, p * other, p)
        q = jnp.where(second, q, q * other)
        t = t * other
    return out, p, q, t


def spread(x, hm):
    return jnp.concatenate([x] * 4, axis=0) * hm


def fold(st):
    f = st[:, 0:128] + st[:, 128:256]
    return jnp.concatenate([f[0:64] + f[64:128], f[128:192] + f[192:256]], axis=0)


def unfold(c, hmf):
    f = jnp.concatenate([c[0:64], c[0:64], c[64:128], c[64:128]], axis=0)
    return jnp.concatenate([f, f], axis=1) * hmf


def head_sum(x, hm):
    hi = x.astype(BF)
    lo = (x - hi.astype(F32)).astype(BF)
    return nn(hi, hm) + nn(lo, hm)


def constants():
    sel = np.zeros((464, 512), np.float32)
    for base, count, off in ((0, 10, 0), (160, 10, 10), (320, 4, 20), (384, 1, 28), (400, 4, 24)):
        for q in range(16):
            for i in range(count):
                sel[base + q * count + i, q * 32 + off + i] = 1
    shmask = np.zeros((8, 160), np.float32)
    for j in range(5):
        shmask[j, 32 * j : 32 * j + 32] = 1
    f = np.arange(256) // 64
    hm = (f[:, None] == f[None, :]).astype(np.float32)
    t = np.arange(64)[:, None]
    u = (np.arange(256) % 64)[None, :]
    lev, levt, sums = [], [], []
    a = np.arange(64)[:, None]
    e = np.arange(64)[None, :]
    for m in (1, 2, 4, 8, 16, 32):
        same = t // (2 * m) == u // (2 * m)
        lev.append(same & (t // m % 2 == 1) & (u // m % 2 == 0))
        levt.append(same & (t // m % 2 == 0) & (u // m % 2 == 1))
        half = a // m == e // m
        sums.append(half & np.where(a // m % 2 == 0, e < a, e > a))
    sums += [e < a, e > a]
    lev = np.stack(lev + levt).astype(np.float32)
    sums = np.concatenate(sums, axis=1).astype(np.float32)
    return (
        jnp.asarray(sel, BF),
        jnp.asarray(shmask, F32),
        jnp.asarray(hm, BF),
        jnp.asarray(lev, F32),
        jnp.asarray(sums, BF),
    )


def layer_kernel(names, *refs):
    R = SimpleNamespace(**dict(zip(names, refs)))
    s, h = place()
    prv, nxt = lax.rem(s + 15, 16), lax.rem(s + 1, 16)
    net = Net(R.ss, R.rs)
    both = (0, 1)
    z1 = jnp.zeros((1, W), F32)

    hid = [HeadGather(net, lambda i, b=b: R.xF.at[b, i]) for b in both]
    smg = HeadGather(net, lambda i: R.smF.at[i])
    midg = [HeadGather(net, lambda i, b=b: R.midF.at[b, i]) for b in both]
    gkvg = [HeadGather(net, lambda i, b=b: R.gF.at[b, i]) for b in both]
    gzg = [HeadGather(net, lambda i, b=b: R.midF.at[b, i]) for b in both]

    def scatter(b, e):
        return HeadScatter(
            net, R.part.at[b], R.fromsib.at[e, b], R.tosend.at[b], R.fromz.at[e, b]
        )

    rs1, rs2, rs3, rs4 = [[scatter(b, e) for b in both] for e in (0, 1, 0, 1)]

    def rows128(ref, q):
        return ref.at[pl.ds(pl.multiple_of(q * 128, 128), 128), :]

    def cols128(ref, q):
        return ref.at[:, pl.ds(pl.multiple_of(q * 128, 128), 128)]

    tws = [
        SeqGather(net, R.tw.at[i], lambda q, i=i: rows128(R.twV.at[i], q), i % 2 == 0, R.ls.at[i])
        for i in range(4)
    ]
    tos = SeqGather(net, R.to, lambda q: cols128(R.toV, q), True, R.ls.at[4])
    cks = SeqGather(net, R.ck, lambda q: rows128(R.ckF, q), True, R.ls.at[5])
    cvs = SeqGather(net, R.cv, lambda q: cols128(R.cvF, q), False, R.ls.at[6])
    crs = SeqGather(net, R.cr, lambda q: rows128(R.crF, q), False, R.ls.at[7])
    sca = SeqScatter(net, R.gaH, R.ra1, R.ra2, R.ra3, True, R.ls.at[8], R.ls.at[20:24])
    scb = SeqScatter(net, R.gbH, R.rb1, R.rb2, R.rb3, False, R.ls.at[9], R.ls.at[24:28])

    def seq_step(k):
        sq, hq = place()
        return lax.rem(sq + k, 16), hq

    smalls = [
        net.copy(lambda k=k: (R.small, R.sm.at[place()[0]], seq_step(k))) for k in range(1, 16)
    ]

    def beside(k, step):
        sq, hq = place()
        return lax.rem(sq + step, 16), lax.rem(hq + k, 8)

    edges = [net.copy(lambda k=k: (R.bsrc, R.bord.at[place()[1]], beside(k, 1))) for k in range(8)]
    cots = {
        (b, k): net.copy(
            lambda b=b, k=k: (
                R.cot.at[b, pl.ds(pl.multiple_of(beside(k, 0)[1] * TC, TC), TC), :],
                R.gch.at[b, place()[1]],
                beside(k, 0),
            )
        )
        for b in both
        for k in range(1, 8)
    }
    last = [net.copy(lambda k=k: (R.bsend.at[beside(k, 0)[1]], R.brecv.at[place()[1]], beside(k, 15))) for k in range(8)]
    rex = [
        net.copy(lambda k=k: (R.rsend, R.rrecv.at[place()[1]], beside(k, 0))) for k in range(1, 8)
    ]
    smo = [
        net.copy(lambda k=k: (R.psend.at[seq_step(k)[0]], R.psrecv.at[place()[0]], seq_step(k)))
        for k in range(1, 16)
    ]

    def mid_border(b, k):
        return pltpu.make_async_remote_copy(
            src_ref=R.mb.at[b],
            dst_ref=R.bmid.at[b],
            send_sem=R.bs.at[b * 8 + k],
            recv_sem=R.br.at[b],
            device_id=(nxt, k),
            device_id_type=MESH,
        )

    def grad_border(b, frm):
        return pltpu.make_async_remote_copy(
            src_ref=R.gsend.at[b],
            dst_ref=R.grecv.at[b, frm],
            send_sem=R.bs.at[16 + b],
            recv_sem=R.br.at[2 + b * 8 + frm],
            device_id=(prv, 7),
            device_id_type=MESH,
        )

    def carry_copy(e, b, dst, frm):
        return pltpu.make_async_remote_copy(
            src_ref=R.csend.at[e, b],
            dst_ref=R.crecv.at[b, frm],
            send_sem=R.cs.at[(2 * e + b) * 16 + dst],
            recv_sem=R.cr_.at[(2 * e + b) * 16 + frm],
            device_id=(dst, h),
            device_id_type=MESH,
        )

    def carry_each(e, b, act):
        def body(i, _):
            act(carry_copy(e, b, i, s))
            return 0

        lo, hi = (s + 1, 16) if e == 0 else (0, s)
        lax.fori_loop(lo, hi, body, 0)

    def carry_send(e, b, state, total):
        R.csend[e, b, 0:128, :] = fold(state).astype(BF)
        R.csend[e, b, 128:144, :] = jnp.concatenate(
            [total[:, 0:128], total[:, 128:256], jnp.zeros((14, 128), F32)], axis=0
        ).astype(BF)
        carry_each(e, b, lambda c: c.start())

    def carry_wait(e, b, hmf):
        R.carry[b] = jnp.zeros((128, 128), F32)

        def body(i, _):
            j = i if e == 0 else 15 - i
            carry_copy(e, b, 0, j).wait_recv()
            tt = R.crecv[b, j, 128:144, :].astype(F32)
            for g in range(2):
                at = slice(g * 64, g * 64 + 64)
                R.carry[b, at, :] = R.carry[b, at, :] * tt[g : g + 1] + R.crecv[b, j, at, :].astype(F32)
            return 0

        lax.fori_loop(0, s if e == 0 else 15 - s, body, 0)
        return unfold(R.carry[b], hmf)

    R.small[...] = jnp.concatenate(
        [a[...].astype(F32) for a in (R.sf, R.s2nd, R.d1st, R.d2nd, R.vectors)]
        + [jnp.zeros((3, W), F32)],
        axis=0,
    ).astype(BF)
    for b in both:
        R.bsrc[16 * b : 16 * b + 16, :] = R.x[b, TB - 16 : TB, :]
        R.xF[b, h] = R.x[b]
    greet(head_peers() + seq_peers() + diagonal_peers(1) + diagonal_peers(15))
    hid[0].start()
    for c in smalls + edges:
        c.start()
    hid[1].start()
    R.sm[s] = R.small[...]
    for c in smalls:
        c.wait_recv()
    for t in tws:
        t.p1()
    comp = nn(R.sel[...], R.sm[...].reshape(512, W)).astype(BF)
    R.smF[h] = comp[0:400]
    R.ds2[...] = comp[400:464]
    smg.start()
    for b in both:
        hid[b].relay()
    for t in tws:
        t.p2()
    tos.p1()
    for b in both:
        hid[b].relay_far()
    smg.relay()
    hid[0].finish()
    n1 = Norm1(R)
    n1.stats(0)
    smg.relay_far()
    hid[1].finish()
    n1.stats(1)
    for c in edges:
        c.wait_recv()
    n1.edge_stats()
    smg.finish()
    vl = R.smF[h, R_VEC : R_VEC + 16, :].astype(F32)
    hmb = R.hm[...]
    hmf = hmb.astype(F32)

    def time_forward(**kw):
        L = SimpleNamespace(**kw)

        def shift(b):
            rows = rows_of(b)
            L.mixacc[...] = jnp.zeros_like(L.mixacc)

            def body(i):
                n, normed, differ, v = n1.block(i, b)
                mixed = (normed + differ * v[2:3]).astype(BF)
                L.mixacc[...] += nt(mixed, R.smF[i, R_FIRST : R_FIRST + 160, :])

            fori(8, body)
            hidden = jnp.tanh(L.mixacc[...])
            R.sh[rows, :] = hidden
            for j in range(5):
                L.shm[j, rows, :] = (hidden * R.shmask[j : j + 1, :]).astype(BF)

        def targets(b):
            rows = rows_of(b)
            L.proj[:, rows, :] = jnp.zeros((4, TB, W), F32)
            L.dacc[...] = jnp.zeros_like(L.dacc)

            def body(i):
                col = pl.ds(pl.multiple_of(i * W, W), W)
                n, normed, differ, v = n1.block(i, b)
                second = R.smF[i, R_SECOND : R_SECOND + 160, :]
                for j in range(5):
                    mix = nn(L.shm[j, rows, :], second)
                    target = (normed + differ * (v[3 + j : 4 + j] + mix)).astype(BF)
                    if j == 0:
                        L.dacc[...] += nt(target, R.smF[i, R_DECAY1 : R_DECAY1 + 64, :])
                    else:
                        L.proj[j - 1, rows, :] += nn(target, R.twV[j - 1, col, :])

            fori(8, body)
            hidden = jnp.tanh(L.dacc[...])
            R.dh[rows, :] = hidden
            ld = -jnp.exp(vl[8:9] + nn(hidden.astype(BF), R.ds2[...]))
            R.logd[rows, :] = ld
            L.wdec[rows, :] = jnp.exp(ld) * R.keep[rows, :]
            R.proj[:, rows, :] = L.proj[:, rows, :].astype(BF)

        def states(b):
            L.st[b] = jnp.zeros((W, W), F32)
            R.tpre[8 + b : 9 + b, :] = jnp.ones((1, W), F32)

            def body(c):
                rows = pl.ds(pl.multiple_of(b * TB + c * C, C), C)
                i = b * 4 + c
                r, k, v = L.proj[2, rows, :], L.proj[0, rows, :], L.proj[1, rows, :]
                lv, p, q, t = tree(r, k, L.wdec[rows, :], R.keep[rows, :])
                for l, (a, e) in enumerate(lv):
                    L.xs[l, rows, :] = (a * e).astype(BF)
                R.rp[rows, :] = (r * p).astype(BF)
                L.starts[i] = L.st[b].astype(BF)
                R.tch[pl.ds(i, 1), :] = t[0:1]
                before = R.tpre[8 + b : 9 + b, :]
                R.tpre[pl.ds(i, 1), :] = before
                R.tpre[8 + b : 9 + b, :] = before * t[0:1]
                L.st[b] = L.st[b] * t[0:1] + nn(v.T.astype(BF), (k * q).astype(BF)) * hmf

            fori(4, body)
            carry_send(0, b, L.st[b], R.tpre[8 + b : 9 + b, :])

        def inner(b):
            def body(c):
                rows = pl.ds(pl.multiple_of(b * TB + c * C, C), C)
                r, k, v = L.proj[2, rows, :], L.proj[0, rows, :], L.proj[1, rows, :]
                a = jnp.zeros((C, W), F32)
                at = jnp.zeros((C, W), F32)
                for l in range(LV):
                    xl = L.xs[l, rows, :]
                    y = nt(xl, spread(xl, hmb))
                    a = a + y * R.levels[l]
                    at = at + y * R.levels[LV + l]
                R.scores[rows, :] = at.astype(BF)
                bonus = head_sum(r * vl[9:10] * k, hmb)
                L.ov[rows, :] = nn(a.astype(BF), spread(v.astype(BF), hmb)) + bonus * v

            fori(4, body)

        def outer(b):
            st = carry_wait(0, b, hmf)
            L.st[b] = st
            if b == 1:
                for g in (cks, crs):
                    g.p2(True)

            def body(c):
                i = b * 4 + c
                rows = pl.ds(pl.multiple_of(b * TB + c * C, C), C)
                start = L.starts[i].astype(F32) + L.st[b] * R.tpre[pl.ds(i, 1), :]
                R.starts[i] = fold(start).astype(BF)
                o = L.ov[rows, :] + nt(R.rp[rows, :], start.astype(BF))
                d = o - head_sum(o, hmb) / 64.0
                sc = lax.rsqrt(head_sum(d * d, hmb) / 64.0 + GEPS)
                gn = d * sc
                R.gnorm[rows, :] = gn
                R.gscale[rows, :] = sc
                g = L.proj[3, rows, :]
                R.gate[rows, :] = (
                    (gn * vl[10:11] + vl[11:12]) * (g * jax.nn.sigmoid(g))
                ).astype(BF)

            fori(4, body)

        def out(b):
            def body(i):
                y = nn(R.gate[rows_of(b), :], R.toV[:, pl.ds(pl.multiple_of(i * W, W), W)])
                R.part[b, :, i] = y.astype(BF).reshape(8, TC, W)

            fori(8, body)
            for k in (2, 1, 3, 0):
                rs1[b].give(k)

        for t in tws:
            t.p3()
        tos.p2()
        shift(0)
        shift(1)
        for t in tws:
            t.finish()
        for g in (cks, crs, cvs):
            g.p0()
        targets(0)
        states(0)
        tos.p3()
        targets(1)
        states(1)
        saved = pltpu.make_async_copy(R.twV, R.twF, R.ls.at[10])
        saved.start()
        inner(0)
        for c in cots.values():
            c.start()
        inner(1)
        outer(0)
        tos.finish()
        out(0)
        outer(1)
        rs1[0].pass_far()
        out(1)
        rs1[0].pass_near()
        rs1[1].pass_far()
        saved.wait()

    f32n = pltpu.VMEM((N, W), F32)
    pl.run_scoped(
        time_forward,
        mixacc=pltpu.VMEM((TB, 160), F32),
        shm=pltpu.VMEM((5, N, 160), BF),
        dacc=pltpu.VMEM((TB, 64), F32),
        proj=pltpu.VMEM((4, N, W), F32),
        wdec=f32n,
        xs=pltpu.VMEM((LV, N, W), BF),
        starts=pltpu.VMEM((8, W, W), BF),
        st=pltpu.VMEM((2, W, W), F32),
        ov=f32n,
    )

    def middle(b):
        m = rs1[b].total() + R.xF[b, :, pl.ds(pl.multiple_of(h * TC, TC), TC), :].astype(F32)
        R.mid[b] = m
        R.midF[b, h] = m.astype(BF)
        for i in range(8):
            R.mb[b, i : i + 1, :] = R.mid[b, i, TC - 1 : TC, :]
        midg[b].start()

        @pl.when(h == 7)
        def _():
            for k in range(8):
                mid_border(b, k).start()

    def channel(**kw):
        L = SimpleNamespace(**kw)
        loads = [
            pltpu.make_async_copy(a, c, R.ls.at[11 + i])
            for i, (a, c) in enumerate(((R.ckF, L.ck), (R.crF, L.cr), (R.cvF, L.cv)))
        ]

        def pairs(i):
            at = pl.ds(pl.multiple_of(lax.rem(i, 4) * N, N), N)
            return R.twV.at[i // 4, at, :], R.twV.at[2 + i // 4, at, :]

        def block(i, b):
            rows = rows_of(b)
            v = R.smF[i, R_VEC : R_VEC + 16, :].astype(F32)
            u = slab_of(R.midF.at[b], i).astype(F32)
            n2 = (u - L.mean[rows, :]) * L.rstd[rows, :] * v[12:13] + v[13:14]
            first = L.bstat[b, pl.ds(i, 1), :] * v[12:13] + v[13:14]
            return n2, shift_down(n2, first, R.keep[rows, :]) - n2, v

        def mixing(b):
            rows = rows_of(b)

            def stat_body(i):
                m, r = row_stats(R.midF[b, i].astype(F32))
                at = pl.ds(pl.multiple_of(b * TB + i * TC, TC), TC)
                L.mean[at, :] = m
                L.rstd[at, :] = r

            fori(8, stat_body)
            mid_border(b, 0).wait_recv()
            e = R.bmid[b]
            m = jnp.sum(jnp.sum(e, axis=0, keepdims=True), axis=1, keepdims=True) / D
            d = e - m
            v = jnp.sum(jnp.sum(d * d, axis=0, keepdims=True), axis=1, keepdims=True) / D
            L.bstat[b] = d * lax.rsqrt(v + EPS)
            if b == 0:
                for c in loads[0:2]:
                    c.wait()
            L.kp[rows, :] = jnp.zeros((TB, FFL), F32)
            L.rec[rows, :] = jnp.zeros((TB, W), F32)

            def body(i):
                at = pl.ds(pl.multiple_of(i * W, W), W)
                n2, d2, v = block(i, b)
                a = (n2 + d2 * v[14:15]).astype(BF)
                c = (n2 + d2 * v[15:16]).astype(BF)
                pk, pr = pairs(i)
                pk[rows, :] = a
                pr[rows, :] = c
                L.kp[rows, :] += nn(a, L.ck[at, :])
                L.rec[rows, :] += nn(c, L.cr[at, :])

            fori(8, body)
            g = jax.nn.sigmoid(L.rec[rows, :])
            L.rec[rows, :] = g
            R.gF[b, h] = (R.cot[b] * g).astype(BF).reshape(8, TC, W)
            gkvg[b].start()

        def hidden_units(b):
            def square(i):
                at = pl.ds(pl.multiple_of(b * TB + i * 64, 64), 64)
                u = L.kp[at, :]
                e = jnp.exp(-jnp.abs(u))
                p = jnp.maximum(u, 0.0) + jnp.log(1.0 + e)
                L.sq[at, :] = (p * p).astype(BF)
                L.kp[at, :] = 2.0 * p * jnp.where(u >= 0, 1.0, e) / (1.0 + e)

            fori(4, square)
            if b == 0:
                cvs.finish()
                loads[2].start()
                loads[2].wait()
            rs1[b].drain()

            def out(i):
                y = nn(L.sq[rows_of(b), :], L.cv[:, pl.ds(pl.multiple_of(i * W, W), W)])
                R.part[b, i] = y.astype(BF).reshape(8, TC, W)

            for k in (2, 1, 3, 0):
                out(rs2[b].theirs(k))
                rs2[b].give(k)
                out(rs2[b].ours(k))

        def key_grad(b):
            rows = rows_of(b)
            gkvg[b].finish()
            L.gs[...] = jnp.zeros_like(L.gs)

            def body(i):
                a = R.gF[b, i].reshape(TB, W)
                L.gs[...] += nt(a, L.cv[:, pl.ds(pl.multiple_of(i * W, W), W)])

            fori(8, body)
            L.gk[rows, :] = (L.gs[...] * L.kp[rows, :]).astype(BF)

        def result(b):
            rows = rows_of(b)
            co = rs2[b].total().reshape(TB, W)
            g = L.rec[rows, :]
            R.result[b] = slab_of(R.midF.at[b], h).astype(F32) + g * co
            L.gr[rows, :] = (R.cot[b] * co * g * (1.0 - g)).astype(BF)

        def back(b):
            rows = rows_of(b)
            rs2[b].drain()
            midg[b].drain()

            def body(i):
                at = pl.ds(pl.multiple_of(i * W, W), W)
                n2, d2, v = block(i, b)
                gpk = nt(L.gk[rows, :], L.ck[at, :])
                gpr = nt(L.gr[rows, :], L.cr[at, :])
                R.vg[i, 2 + 2 * b : 3 + 2 * b, :] = jnp.sum(gpk * d2, axis=0, keepdims=True)
                R.vg[i, 3 + 2 * b : 4 + 2 * b, :] = jnp.sum(gpr * d2, axis=0, keepdims=True)
                gd = gpk * v[14:15] + gpr * v[15:16]
                kg = gd * R.keep[rows, :]
                R.gsend[b, pl.ds(i, 1), :] = kg[0:1]
                y = gpk + gpr - gd + shift_up(kg)
                R.part[b, :, i] = y.astype(BF).reshape(8, TC, W)

            fori(8, body)
            for k in (2, 1, 3, 0):
                rs3[b].give(k)
            grad_border(b, h).start()

        def norm_back(b):
            u = R.mid[b]
            m, r = row_stats(u)
            n2 = (u - m[None]) * r[None]
            L.gout[...] = rs3[b].total()

            @pl.when(h == 7)
            def _():
                for i in range(8):
                    grad_border(b, i).wait_recv()
                t = jnp.sum(R.grecv[b], axis=0)
                for i in range(8):
                    L.gout[i, TC - 1 : TC, :] += t[i : i + 1]

            go = L.gout[...]
            gain = R.smF[:, R_VEC + 12 : R_VEC + 13, :].astype(F32)
            v12 = jnp.sum(go * n2, axis=1, keepdims=True)
            v13 = jnp.sum(go, axis=1, keepdims=True)
            if b == 0:
                R.vg[:, 0:1, :] = v12
                R.vg[:, 1:2, :] = v13
            else:
                R.vg[:, 0:1, :] += v12
                R.vg[:, 1:2, :] += v13
            gn = go * gain
            ma = jnp.sum(jnp.sum(gn, axis=0), axis=1, keepdims=True) / D
            mb = jnp.sum(jnp.sum(gn * n2, axis=0), axis=1, keepdims=True) / D
            R.midF[b, h] = (R.gch[b] + (gn - ma[None] - n2 * mb[None]) * r[None]).astype(BF)
            gzg[b].start()

        def staged(home, rows, xfirst, sem, make):
            def copies(i):
                got = []
                for e in range(2):
                    q = 2 * i + e
                    if not xfirst:
                        q = lax.rem(q, 4) * 4 + q // 4
                    at = lax.rem(i, 2)
                    got.append(
                        pltpu.make_async_copy(
                            L.stage.at[at, e, 0:rows], home.at[q], R.ls.at[sem + 2 * at + e]
                        )
                    )
                return got

            def body(i):
                @pl.when(i >= 2)
                def _():
                    for c in copies(i - 2):
                        c.wait()

                y = make(i)
                for e in range(2):
                    at = 0
                    for t in y:
                        L.stage[lax.rem(i, 2), e, at : at + t.shape[0], :] = t[
                            :, 128 * e : 128 * e + 128
                        ].astype(BF)
                        at += t.shape[0]
                for c in copies(i):
                    c.start()

            fori(8, body)
            for i in (6, 7):
                for c in copies(i):
                    c.wait()

        def value_weight():
            L.tr[...] = L.sq[...].T
            staged(
                R.gbH, FFL, False, 28, lambda i: [nn(L.tr[...], R.gF[:, i].reshape(N, W))]
            )

        def key_weight():
            L.tr[...] = L.gk[...].T
            L.grT[...] = L.gr[...].T

            def make(i):
                pk, pr = pairs(i)
                return [nn(L.tr[...], pk[...]), nn(L.grT[...], pr[...])]

            staged(R.gaH, FFL + W, True, 32, make)

        middle(0)
        rs1[1].pass_near()
        for g in (cks, crs):
            g.p3()
        midg[0].relay()
        midg[0].relay_far()
        middle(1)
        cvs.p2(True)
        for g in (cks, crs):
            g.finish()
        for c in loads[0:2]:
            c.start()
        for t in tws:
            t.drain()
        midg[0].finish()
        midg[1].relay()
        mixing(0)
        midg[1].relay_far()
        midg[1].finish()
        gkvg[0].relay()
        cvs.p3()
        mixing(1)
        gkvg[0].relay_far()
        hidden_units(0)
        gkvg[1].relay()
        rs2[0].pass_far()
        gkvg[1].relay_far()
        key_grad(0)
        rs2[0].pass_near()
        hidden_units(1)
        rs2[1].pass_far()
        result(0)
        back(0)
        rs2[1].pass_near()
        key_grad(1)
        rs3[0].pass_far()
        value_weight()
        result(1)
        rs3[0].pass_near()
        back(1)
        for c in cots.values():
            c.wait_recv()
        scb.near()
        scb.own().start()
        norm_back(0)
        rs3[1].pass_far()
        key_weight()
        sca.near()
        sca.own().start()
        gzg[0].relay()
        rs3[1].pass_near()
        gzg[0].relay_far()
        norm_back(1)

    for b in both:
        R.gch[b, h] = R.cot[b, pl.ds(pl.multiple_of(h * TC, TC), TC), :]
    pl.run_scoped(
        channel,
        ck=pltpu.VMEM((D, FFL), BF),
        cv=pltpu.VMEM((FFL, D), BF),
        cr=pltpu.VMEM((D, W), BF),
        mean=pltpu.VMEM((N, 1), F32),
        rstd=pltpu.VMEM((N, 1), F32),
        bstat=pltpu.VMEM((2, 8, W), F32),
        kp=pltpu.VMEM((N, FFL), F32),
        rec=f32n,
        sq=pltpu.VMEM((N, FFL), BF),
        gk=pltpu.VMEM((N, FFL), BF),
        gr=pltpu.VMEM((N, W), BF),
        gs=pltpu.VMEM((TB, FFL), F32),
        tr=pltpu.VMEM((FFL, N), BF),
        grT=pltpu.VMEM((W, N), BF),
        gout=pltpu.VMEM((8, TC, W), F32),
        stage=pltpu.VMEM((2, 2, FFL + W, 128), BF),
    )

    def time_backward(**kw):
        O = SimpleNamespace(**kw)
        sea = SeqScatter(net, O.ea, R.ea1, O.ea2, R.ea3, True)
        seb = SeqScatter(net, O.eb, R.eb1, O.eb2, R.eb3, False)
        O.shT[...] = R.sh[...].T.astype(BF)
        for b in both:
            gkvg[b].drain()

        def shm(j, rows):
            return (R.sh[rows, :] * R.shmask[j : j + 1, :]).astype(BF)

        def wkv_backward(**kw):
            L = SimpleNamespace(**kw)

            def gated(b):
                rows = rows_of(b)
                L.gated[rows, :] = jnp.zeros((TB, W), F32)

                def body(i):
                    a = slab_of(R.midF.at[b], i)
                    L.gated[rows, :] += nt(a, R.toV[:, pl.ds(pl.multiple_of(i * W, W), W)])

                fori(8, body)

                def gate_body(i, acc):
                    at = pl.ds(pl.multiple_of(b * TB + i * 64, 64), 64)
                    gd = L.gated[at, :]
                    gn = R.gnorm[at, :]
                    g = R.proj[3, at, :].astype(F32)
                    sg = jax.nn.sigmoid(g)
                    gno = gd * (g * sg)
                    dg = gd * (gn * vl[10:11] + vl[11:12]) * sg * (1.0 + g * (1.0 - sg))
                    O.gp[3, at, :] = dg.astype(BF)
                    gg = gno * vl[10:11]
                    ma = head_sum(gg, hmb) / 64.0
                    mb = head_sum(gg * gn, hmb) / 64.0
                    L.go[at, :] = R.gscale[at, :] * (gg - ma - gn * mb)
                    return (
                        acc[0] + jnp.sum(gno * gn, axis=0, keepdims=True),
                        acc[1] + jnp.sum(gno, axis=0, keepdims=True),
                    )

                return lax.fori_loop(0, 4, gate_body, (z1, z1))

            def adjoint(b):
                L.ds[b] = jnp.zeros((W, W), F32)
                L.tsuf[8 + b : 9 + b, :] = jnp.ones((1, W), F32)

                def body(e):
                    i = b * 4 + 3 - e
                    rows = pl.ds(pl.multiple_of(i * C, C), C)
                    L.dsl[i] = L.ds[b].astype(BF)
                    t = R.tch[pl.ds(i, 1), :]
                    after = L.tsuf[8 + b : 9 + b, :]
                    L.tsuf[pl.ds(i, 1), :] = after
                    L.tsuf[8 + b : 9 + b, :] = after * t
                    L.ds[b] = L.ds[b] * t + nn(L.go[rows, :].T.astype(BF), R.rp[rows, :]) * hmf

                fori(4, body)
                carry_send(1, b, L.ds[b], L.tsuf[8 + b : 9 + b, :])

            def output_weight():
                L.gatT[...] = R.gate[...].T

                def body(i):
                    a = R.midF[:, :, i].reshape(N, W)
                    put(O.eb, i, 0, nn(L.gatT[...], a).astype(BF), False)

                fori(8, body)

            def gate_weight():
                O.gpT[3] = O.gp[3].T

                def body(i):
                    y = jnp.zeros((W, W), F32)
                    for b in both:
                        rows = rows_of(b)
                        n, normed, differ, v = n1.block(i, b)
                        mix = nn(shm(4, rows), R.smF[i, R_SECOND : R_SECOND + 160, :])
                        target = (normed + differ * (v[7:8] + mix)).astype(BF)
                        y = y + nn(O.gpT[3, :, rows], target)
                    put(O.ea, i, 0, y.astype(BF), True)

                fori(8, body)

            def inner(b, gu):
                def body(c, gu):
                    rows = pl.ds(pl.multiple_of(b * TB + c * C, C), C)
                    r, k, v = [R.proj[j, rows, :].astype(F32) for j in (2, 0, 1)]
                    g, kp = L.go[rows, :], R.keep[rows, :]
                    lv, p, q, t = tree(r, k, jnp.exp(R.logd[rows, :]) * kp, kp)
                    L.pP[rows, :] = p
                    L.pQ[rows, :] = q
                    vb, gb = v.astype(BF), g.astype(BF)
                    gsp = spread(gb, hmb)
                    da = nt(gb, spread(vb, hmb))
                    dat = nt(vb, gsp)
                    row = iota((C, W), 0)
                    agr = jnp.zeros((C, W), F32)
                    agk = jnp.zeros((C, W), F32)
                    ys = []
                    for l, (a, e) in enumerate(lv):
                        x = (a * e).astype(BF)
                        d = (da * R.levels[l] + dat * R.levels[LV + l]).astype(BF)
                        gx = nn(d, spread(x, hmb))
                        second = (row // (1 << l)) % 2 == 1
                        ge = gx * e
                        agr = agr + jnp.where(second, ge, 0.0)
                        agk = agk + jnp.where(second, 0.0, ge)
                        ys.append((x.astype(F32) * gx).astype(BF))
                    L.gG[rows, :] = nn(R.sums[:, 0 : LV * C], jnp.concatenate(ys, axis=0))
                    u = vl[9:10]
                    dad = head_sum(g * v, hmb)
                    bonus = head_sum(r * u * k, hmb)
                    L.gr[rows, :] = agr + u * k * dad
                    L.gk[rows, :] = agk + u * r * dad
                    L.gv[rows, :] = nn(R.scores[rows, :], gsp) + bonus * g
                    return gu + jnp.sum(r * k * dad, axis=0, keepdims=True)

                return lax.fori_loop(0, 4, body, gu)

            def outer(b, g8):
                L.ds[b] = carry_wait(1, b, hmf)

                def body(c, g8):
                    i = b * 4 + c
                    rows = pl.ds(pl.multiple_of(i * C, C), C)
                    st = unfold(R.starts[i].astype(F32), hmf)
                    de = L.dsl[i].astype(F32) + L.ds[b] * L.tsuf[pl.ds(i, 1), :]
                    deb = de.astype(BF)
                    p, q = L.pP[rows, :], L.pQ[rows, :]
                    kq = (R.proj[0, rows, :].astype(F32) * q).astype(BF)
                    rpc = R.rp[rows, :]
                    gkq = nn(R.proj[1, rows, :], deb)
                    grp = nn(L.go[rows, :].astype(BF), st.astype(BF))
                    O.gp[1, rows, :] = (L.gv[rows, :] + nt(kq, deb)).astype(BF)
                    O.gp[0, rows, :] = (L.gk[rows, :] + gkq * q).astype(BF)
                    O.gp[2, rows, :] = (L.gr[rows, :] + grp * p).astype(BF)
                    ky = (kq.astype(F32) * gkq).astype(BF)
                    ry = (rpc.astype(F32) * grp).astype(BF)
                    cst = jnp.sum(st * de, axis=0, keepdims=True) * R.tch[pl.ds(i, 1), :]
                    gl = nn(R.sums[:, LV * C :], jnp.concatenate([ky, ry], axis=0))
                    gw = (L.gG[rows, :] + gl + cst) * R.logd[rows, :]
                    O.gw[rows, :] = gw.astype(BF)
                    return g8 + jnp.sum(gw, axis=0, keepdims=True)

                return lax.fori_loop(0, 4, body, g8)

            gzg[0].finish()
            gzg[1].relay()
            a10, a11 = gated(0)
            adjoint(0)
            gzg[1].relay_far()
            gzg[1].finish()
            b10, b11 = gated(1)
            adjoint(1)
            sca.far()
            scb.far()
            output_weight()
            seb.near()
            seb.far()
            g9 = inner(0, z1)
            gate_weight()
            sea.near()
            sea.far()
            g9 = inner(1, g9)
            scb.p2([L.stage.at[0, :, 0:FFL], L.stage.at[1, :, 0:FFL]])
            g8 = outer(0, z1)
            sca.p2([L.stage.at[0], L.stage.at[1]])
            g8 = outer(1, g8)
            R.gvec[0:1, :] = g8
            R.gvec[1:2, :] = g9
            R.gvec[2:3, :] = a10 + b10
            R.gvec[3:4, :] = a11 + b11

        reload = pltpu.make_async_copy(R.twF, R.twV, R.ls.at[10])
        reload.start()
        pl.run_scoped(
            wkv_backward,
            gated=f32n,
            go=f32n,
            gr=f32n,
            gk=f32n,
            gv=f32n,
            gG=f32n,
            pP=f32n,
            pQ=f32n,
            dsl=pltpu.VMEM((8, W, W), BF),
            ds=pltpu.VMEM((2, W, W), F32),
            tsuf=pltpu.VMEM((16, W), F32),
            gatT=pltpu.VMEM((W, N), BF),
            stage=pltpu.VMEM((2, 3, FFL + W, 128), BF),
        )

        for j in range(3):
            O.gpT[j] = O.gp[j].T
        dhv = R.dh[...]
        gdv = nt(O.gw[...], R.ds2[...]) * (1.0 - dhv * dhv)
        O.gdp[...] = gdv.astype(BF)
        O.gdpT[...] = gdv.T.astype(BF)
        O.lsm[400:464, :] = nn(dhv.T.astype(BF), O.gw[...])
        reload.wait()

        def normed_back(**kw):
            L = SimpleNamespace(**kw)
            sta = SeqScatter(net, L.ta, R.ta1, L.ta2, R.ta3, True)
            stb = SeqScatter(net, L.tb, R.tb1, L.tb2, R.tb3, False)
            sms = HeadScatter(net, L.sg, R.sgsib, L.sgsend, R.sgz)
            L.gsh[...] = jnp.zeros_like(L.gsh)
            rank = iota((160, W), 0)

            def target_body(i):
                at = pl.ds(pl.multiple_of(i * W, W), W)
                second = R.smF[i, R_SECOND : R_SECOND + 160, :]
                dfirst = R.smF[i, R_DECAY1 : R_DECAY1 + 64, :]
                ws = [jnp.zeros((W, W), F32) for _ in range(3)]
                gsec = jnp.zeros((160, W), F32)
                gd1 = jnp.zeros((64, W), F32)
                rowsum = [z1] * 5
                for b in both:
                    rows = rows_of(b)
                    n, normed, differ, v = n1.block(i, b)
                    a1 = jnp.zeros((TB, W), F32)
                    a2 = jnp.zeros((TB, W), F32)
                    for j in range(5):
                        m = v[3 + j : 4 + j] + nn(shm(j, rows), second)
                        if j < 4:
                            target = (normed + differ * m).astype(BF)
                        if j == 0:
                            gt = nn(O.gdp[rows, :], dfirst)
                            gd1 = gd1 + nn(O.gdpT[:, rows], target)
                        else:
                            gt = nt(O.gp[j - 1, rows, :], R.twV[j - 1, at, :])
                            if j < 4:
                                ws[j - 1] = ws[j - 1] + nn(O.gpT[j - 1, :, rows], target)
                        a1 = a1 + gt
                        a2 = a2 + gt * m
                        qv = gt * differ
                        rowsum[j] = rowsum[j] + jnp.sum(qv, axis=0, keepdims=True)
                        qb = qv.astype(BF)
                        gsec = gsec + jnp.where(rank // 32 == j, nn(O.shT[:, rows], qb), 0.0)
                        L.gsh[rows, :] += nt(qb, second) * R.shmask[j : j + 1, :]
                    L.s1[i, rows, :] = a1.astype(BF)
                    R.gF[b, i] = a2.astype(BF).reshape(8, TC, W)
                put(L.ta, i, 0, ws[0].astype(BF), True)
                put(L.tb, i, 0, ws[1].astype(BF), False)
                put(L.ta, i, W, ws[2][0:128].astype(BF), True)
                put(L.tb, i, W, ws[2][128:256].astype(BF), False)
                L.sg[i, R_SECOND : R_SECOND + 160, :] = gsec.astype(BF)
                L.sg[i, R_DECAY1 : R_DECAY1 + 64, :] = gd1.astype(BF)
                for j in range(5):
                    L.psm[i, 3 + j : 4 + j, :] = rowsum[j]

            fori(8, target_body)
            sea.p2()
            seb.p2()
            sta.near()
            stb.near()
            hidden = R.sh[...]
            gs2 = L.gsh[...] * (1.0 - hidden * hidden)
            L.gshp[...] = gs2.astype(BF)
            L.gshpT[...] = gs2.T.astype(BF)
            L.rsum[...] = jnp.zeros_like(L.rsum)
            lane = iota((TB, 128), 1)

            def mixed_back(b):
                rows = rows_of(b)

                def body(i):
                    first = R.smF[i, R_FIRST : R_FIRST + 160, :]
                    n, normed, differ, v = n1.block(i, b)
                    mixed = (normed + differ * v[2:3]).astype(BF)
                    gm = nn(L.gshp[rows, :], first)
                    gf = nn(L.gshpT[:, rows], mixed)
                    g2 = jnp.sum(gm * differ, axis=0, keepdims=True)
                    gd = R.gF[b, i].reshape(TB, W).astype(F32) + gm * v[2:3]
                    kg = gd * R.keep[rows, :]
                    R.bsend[i, b : b + 1, :] = kg[0:1]
                    gn = L.s1[i, rows, :].astype(F32) + gm - gd + shift_up(kg)
                    R.part[b, i] = gn.astype(BF).reshape(8, TC, W)
                    gg = gn * v[0:1]
                    ra = jnp.sum(gg, axis=1, keepdims=True)
                    rb = jnp.sum(gg * n, axis=1, keepdims=True)
                    L.rsum[rows, :] += jnp.where(lane == 0, ra, jnp.where(lane == 1, rb, 0.0))
                    if b == 0:
                        L.sg[i, R_FIRST : R_FIRST + 160, :] = gf.astype(BF)
                        L.psm[i, 2:3, :] = g2
                    else:
                        had = L.sg[i, R_FIRST : R_FIRST + 160, :].astype(F32)
                        L.sg[i, R_FIRST : R_FIRST + 160, :] = (had + gf).astype(BF)
                        vg = R.vg[i]
                        L.sg[i, R_VEC : R_VEC + 16, :] = jnp.concatenate(
                            [
                                jnp.zeros((2, W), F32),
                                L.psm[i, 2:3, :] + g2,
                                L.psm[i, 3:8, :],
                                jnp.zeros((4, W), F32),
                                vg[0:2],
                                vg[2:4] + vg[4:6],
                            ],
                            axis=0,
                        ).astype(BF)

                fori(8, body)
                for k in (2, 1, 3, 0):
                    rs4[b].give(k)

            for b in both:
                rs3[b].drain()
            R.bsend[...] = jnp.zeros_like(R.bsend)
            mixed_back(0)
            mixed_back(1)
            for c in last:
                c.start()
            sta.far()
            stb.far()
            rs4[0].pass_far()
            for k in (2, 1, 3, 0):
                sms.give(k)
            sca.finish(R.oca)
            scb.finish(R.ocb)
            rs4[0].pass_near()
            rs4[1].pass_far()
            sea.finish(R.oea)
            seb.finish(R.oeb)
            for c in last:
                c.wait_recv()
            edge = jnp.sum(R.brecv[...], axis=0)
            lane8 = iota((1, 128), 1)
            for b in both:
                at = slice(b * TB + TB - 16, b * TB + TB)
                n = (R.xF[b, h, TB - 16 : TB, :].astype(F32) - R.mean[at, :]) * R.rstd[at, :]
                e = edge[b : b + 1] * vl[0:1]
                ra = jnp.sum(e, axis=1, keepdims=True)
                rb = jnp.sum(e * n[15:16], axis=1, keepdims=True)
                end = slice(b * TB + TB - 1, b * TB + TB)
                L.rsum[end, :] += jnp.where(lane8 == 0, ra, jnp.where(lane8 == 1, rb, 0.0))
            R.rsend[...] = L.rsum[...].T[0:8]
            R.rrecv[h] = R.rsend[...]
            for c in rex:
                c.start()
            rs4[1].pass_near()
            sms.pass_far()
            sta.p2()
            stb.p2()
            for c in rex:
                c.wait_recv()
            tot = jnp.sum(R.rrecv[...], axis=0)
            L.rsum[...] = jnp.concatenate([tot, jnp.zeros((120, N), F32)], axis=0).T / D
            sms.pass_near()
            g0, g1 = z1, z1
            for b in both:
                rows = rows_of(b)
                R.mid[b] = rs4[b].total()
                R.mid[b, 7, TC - 1 : TC, :] += edge[b : b + 1]
                gl = R.mid[b].reshape(TB, W)
                n = (R.xF[b, h].astype(F32) - R.mean[rows, :]) * R.rstd[rows, :]
                g0 = g0 + jnp.sum(gl * n, axis=0, keepdims=True)
                g1 = g1 + jnp.sum(gl, axis=0, keepdims=True)
                R.hgrad[b] = slab_of(R.midF.at[b], h).astype(F32) + R.rstd[rows, :] * (
                    gl * vl[0:1] - L.rsum[rows, 0:1] - n * L.rsum[rows, 1:2]
                )
            O.lsm[0:400, :] = sms.total()
            O.lsm[R_VEC : R_VEC + 2, :] += jnp.concatenate([g0, g1], axis=0)
            O.lsm[R_VEC + 8 : R_VEC + 12, :] += R.gvec[0:4, :]
            R.psend[...] = (
                lax.dot_general(R.sel[...], O.lsm[...].astype(BF), (((0,), (0,)), ((), ())), preferred_element_type=F32).astype(BF).reshape(16, 32, W)
            )
            for c in smo:
                c.start()
            R.psrecv[s] = R.psend[s]
            for c in smo:
                c.wait_recv()
            R.osm[...] = jnp.sum(R.psrecv[...].astype(F32), axis=0)
            sta.finish(R.ota)
            stb.finish(R.otb)
            net.drain()

        RT = W + 128
        pl.run_scoped(
            normed_back,
            s1=pltpu.VMEM((8, N, W), BF),
            ta=pltpu.VMEM((16, RT, 128), BF),
            tb=pltpu.VMEM((16, RT, 128), BF),
            ta2=pltpu.VMEM((4, RT, 128), BF),
            tb2=pltpu.VMEM((4, RT, 128), BF),
            sg=pltpu.VMEM((8, 400, W), BF),
            sgsend=pltpu.VMEM((3, 400, W), BF),
            gsh=pltpu.VMEM((N, 160), F32),
            gshp=pltpu.VMEM((N, 160), BF),
            gshpT=pltpu.VMEM((160, N), BF),
            rsum=pltpu.VMEM((N, 128), F32),
            psm=pltpu.VMEM((8, 8, W), F32),
        )

    pl.run_scoped(
        time_backward,
        ea=pltpu.VMEM((16, W, 128), BF),
        eb=pltpu.VMEM((16, W, 128), BF),
        ea2=pltpu.VMEM((4, W, 128), BF),
        eb2=pltpu.VMEM((4, W, 128), BF),
        shT=pltpu.VMEM((160, N), BF),
        gp=pltpu.VMEM((4, N, W), BF),
        gpT=pltpu.VMEM((4, W, N), BF),
        gw=pltpu.VMEM((N, W), BF),
        gdp=pltpu.VMEM((N, 64), BF),
        gdpT=pltpu.VMEM((64, N), BF),
        lsm=pltpu.VMEM((464, W), F32),
    )
    for b in both:

        @pl.when(h == 7)
        def _():
            for k in range(8):
                mid_border(b, k).wait_send()

        grad_border(b, h).wait_send()
        for e in both:
            carry_each(e, b, lambda c: c.wait_send())


def put(ref, i, row, y, xfirst):
    for e in range(2):
        q = 2 * i + e
        if not xfirst:
            q = lax.rem(q, 4) * 4 + q // 4
        ref[q, row : row + y.shape[0], :] = y[:, 128 * e : 128 * e + 128]


VM = pl.BlockSpec(memory_space=pltpu.VMEM)
HB = pl.BlockSpec(memory_space=pl.ANY)
SD = jax.ShapeDtypeStruct


def run_layer(ins):
    far = ("tw", "to", "ck", "cv", "cr")
    RA, RB, RT = FFL + W, FFL, W + 128
    outs = dict(
        result=((2, TB, W), F32, VM),
        hgrad=((2, TB, W), F32, VM),
        oca=((RA, 128), F32, VM),
        ocb=((RB, 128), F32, VM),
        oea=((W, 128), F32, VM),
        oeb=((W, 128), F32, VM),
        ota=((RT, 128), F32, VM),
        otb=((RT, 128), F32, VM),
        osm=((32, W), F32, VM),
        twF=((4, D, W), BF, HB),
        ckF=((D, FFL), BF, HB),
        cvF=((FFL, D), BF, HB),
        crF=((D, W), BF, HB),
        gaH=((16, RA, 128), BF, HB),
        gbH=((16, RB, 128), BF, HB),
        ra1=((3, 4, RA, 128), BF, HB),
        rb1=((3, 4, RB, 128), BF, HB),
    )
    scr = dict(
        small=((32, W), BF),
        sm=((16, 32, W), BF),
        bsrc=((32, W), BF),
        xF=((2, 8, TB, W), BF),
        bord=((8, 32, W), BF),
        smF=((8, 400, W), BF),
        ds2=((64, W), BF),
        twV=((4, D, W), BF),
        toV=((W, D), BF),
        midF=((2, 8, 8, TC, W), BF),
        mid=((2, 8, TC, W), F32),
        mb=((2, 8, W), F32),
        bmid=((2, 8, W), F32),
        gch=((2, 8, TC, W), F32),
        gF=((2, 8, 8, TC, W), BF),
        mean=((N, 1), F32),
        rstd=((N, 1), F32),
        bmean=((32, 1), F32),
        brstd=((32, 1), F32),
        sh=((N, 160), F32),
        dh=((N, 64), F32),
        proj=((4, N, W), BF),
        logd=((N, W), F32),
        gnorm=((N, W), F32),
        gscale=((N, W), F32),
        scores=((N, W), BF),
        starts=((8, 128, 128), BF),
        rp=((N, W), BF),
        gate=((N, W), BF),
        tch=((8, W), F32),
        tpre=((16, W), F32),
        carry=((2, 128, 128), F32),
        csend=((2, 2, 144, 128), BF),
        crecv=((2, 16, 144, 128), BF),
        part=((2, 8, 8, TC, W), BF),
        tosend=((2, 3, 8, TC, W), BF),
        fromsib=((2, 2, 4, 8, TC, W), BF),
        fromz=((2, 2, 3, 8, TC, W), BF),
        gsend=((2, 8, W), F32),
        grecv=((2, 8, 8, W), F32),
        vg=((8, 8, W), F32),
        gvec=((8, W), F32),
        bsend=((8, 8, W), F32),
        brecv=((8, 8, W), F32),
        rsend=((8, N), F32),
        rrecv=((8, 8, N), F32),
        sgsib=((4, 400, W), BF),
        sgz=((3, 400, W), BF),
        psend=((16, 32, W), BF),
        psrecv=((16, 32, W), BF),
        ra2=((4, RA, 128), BF),
        ra3=((3, RA, 128), BF),
        rb2=((4, RB, 128), BF),
        rb3=((3, RB, 128), BF),
        ea1=((3, 4, W, 128), BF),
        ea3=((3, W, 128), BF),
        eb1=((3, 4, W, 128), BF),
        eb3=((3, W, 128), BF),
        ta1=((3, 4, RT, 128), BF),
        ta3=((3, RT, 128), BF),
        tb1=((3, 4, RT, 128), BF),
        tb3=((3, RT, 128), BF),
    )
    sems = dict(ss=430, rs=430, ls=36, bs=18, br=18, cs=64, cr_=64)
    names = list(ins) + list(outs) + list(scr) + list(sems)
    got = pl.pallas_call(
        functools.partial(layer_kernel, names),
        out_shape=[SD(a, t) for a, t, _ in outs.values()],
        in_specs=[HB if k in far else VM for k in ins],
        out_specs=[m for _, _, m in outs.values()],
        scratch_shapes=[pltpu.VMEM(a, t) for a, t in scr.values()]
        + [pltpu.SemaphoreType.DMA((n,)) for n in sems.values()],
        name="layer",
        compiler_params=pltpu.CompilerParams(
            collective_id=1, has_side_effects=True, vmem_limit_bytes=VMEM_LIMIT
        ),
    )(*ins.values())
    return SimpleNamespace(**dict(zip(outs, got)))


def on_device(
    hidden, cotangent, opening_flags, vectors, shift_first, shift_second, decay_first, decay_second,
    time_weights, time_output, channel_key, channel_value, channel_recept,
):
    sel, shmask, hm, levels, sums = constants()
    o = run_layer(
        dict(
            x=hidden,
            cot=cotangent,
            keep=(1.0 - opening_flags.astype(F32)).reshape(N, 1),
            sf=shift_first[0],
            s2nd=shift_second[0],
            d1st=decay_first[0],
            d2nd=decay_second[0],
            vectors=vectors[0],
            sel=sel,
            shmask=shmask,
            hm=hm,
            levels=levels,
            sums=sums,
            tw=time_weights[0],
            to=time_output[0],
            ck=channel_key[0],
            cv=channel_value[0],
            cr=channel_recept[0],
        )
    )
    return finish(o.result, o.hgrad, o.oca, o.ocb, o.oea, o.oeb, o.ota, o.otb, o.osm)


def finish_kernel(
    result, hg, ca, cb, ea, eb, ta, tb, sm,
    o_result, o_hidden, o_vec, o_first, o_second, o_decay1, o_decay2, o_time, o_out, o_key, o_value,
    o_recept,
):
    o_result[...] = result[...]
    o_hidden[...] = hg[...]
    o_first[0] = sm[0:10]
    o_second[0] = sm[10:20]
    o_decay1[0] = sm[20:24]
    o_decay2[0] = sm[24:28]
    o_vec[0] = sm[28:29]
    o_time[0, 0] = ta[0:W].T
    o_time[0, 1] = tb[0:W].T
    o_time[0, 2, :, 0:128] = ta[W:].T
    o_time[0, 2, :, 128:256] = tb[W:].T
    o_time[0, 3] = ea[...].T
    o_out[0] = eb[...]
    o_key[0] = ca[0:FFL].T
    o_value[0] = cb[...]
    o_recept[0] = ca[FFL:].T


def finish(*ins):
    shapes = [
        (2, TB, W), (2, TB, W), (1, 1, W), (1, 10, W), (1, 10, W), (1, 4, W), (1, 4, W),
        (1, 4, 128, W), (1, W, 128), (1, 128, FFL), (1, FFL, 128), (1, 128, W),
    ]
    return pl.pallas_call(
        finish_kernel,
        out_shape=[SD(q, F32) for q in shapes],
        in_specs=[VM] * len(ins),
        out_specs=[VM] * len(shapes),
        name="finish",
        compiler_params=pltpu.CompilerParams(vmem_limit_bytes=VMEM_LIMIT),
    )(*ins)


def solution(mesh):
    last = P(None, "seq", "head")
    turned = P(None, "head", "seq")
    four = P(None, None, "seq", "head")
    return jax.shard_map(
        on_device,
        mesh=mesh,
        in_specs=(last, last, P(None, "seq"), last, last, last, last, last, four, turned, last, turned, last),
        out_specs=(last, last, last, last, last, last, last, four, turned, last, turned, last),
        check_vma=False,
    )
```

profile of v0, /device:TPU:1, one launch (start us, length us, event | category | flops | bytes accessed | tf_op | source)
XLA Modules:
  0.0 317.2 jit_solution(13879266776656510546)
XLA Ops:
  0.6 0.7 subtract_bitcast_fusion
  1.3 0.9 copy.36
  2.2 308.9 %layer.1 = (f32[2,256,256]{2,1,0:T(8,128)}, f32[2,256,256]{2,1,0:T(8,128)}, f32[1152,128]{1,0:T(8,128)}, f32[896,128]{1,0:T(8,128)}, f32[256,128]{1,0:T(8,128)},...) custom-call(bf16[2,256,256]{2,1,0:T(8,128)(2,1)} %refs_0_.1, ...), custom_call_target="tpu_custom_call" | custom-call | tf_op jit(solution)/shard_map/layer/pallas_call | solution.py:1695
  311.1 3.5 %finish.1 = (f32[2,256,256]{2,1,0:T(8,128)}, f32[2,256,256]{2,1,0:T(8,128)}, f32[1,1,256]{2,1,0:T(1,128)}, f32[1,10,256]{2,1,0:T(8,128)}, f32[1,10,256]{2,1,0:T(...) custom-call(f32[2,256,256]{2,1,0:T(8,128)} %get-tuple-element.21.res, ...), custom_call_target="tpu_custom_call" | custom-call | tf_op jit(solution)/shard_map/finish/pallas_call | solution.py:1768
  314.6 1.3 copy.33
  315.9 1.3 copy.34
  (1 shorter events, 0.0 us)
where the time goes:
time: 318 us; the launch traced here: 317 us
  Pallas kernels  312 us (98%)
  local copies, waits for them, and re-layouts  3.52 us (1%)
    pallas_call x1, Pallas kernels, run_layer(): pl.pallas_call(functools.partial(layer_kernel, names), out_shape=[SD(a, t...  309 us

commit v1 on v0

--- a/solution.py
+++ b/solution.py
@@ -329,21 +329,28 @@
 
 
 class SeqScatter:
-    def __init__(self, net, src, recv, acc, recv2, xfirst, own_sem=None, sems=None):
+    def __init__(self, net, src, recv, acc, recv2, tmp, xfirst, own_sem=None, sems=None):
         self.net, self.src, self.recv, self.acc, self.recv2 = net, src, recv, acc, recv2
-        self.xfirst, self.own_sem, self.sems = xfirst, own_sem, sems
+        self.tmp, self.xfirst, self.own_sem, self.sems = tmp, xfirst, own_sem, sems
         f = xfirst
-        self.c1 = {
-            k: net.copy(
-                lambda k=k: (src.at[pl.ds(self.line(0, k) * 4, 4)], recv.at[k - 1], seq_dev(f, k, 0))
+
+        def copy(k, at, to, dst, step):
+            return net.copy(
+                lambda: (self.slots(k, at), recv.at[to, dst : dst + 2], seq_dev(f, step, 0))
             )
-            for k in ORDER
-        }
+
+        self.fa, self.fb = copy(2, 0, 2, 0, 1), copy(2, 2, 2, 2, 3)
+        self.ub, self.da = copy(1, 2, 0, 2, 1), copy(3, 0, 1, 0, 3)
+        self.ua = net.copy(lambda: (self.tmp.at[0], recv.at[0, 0:2], seq_dev(f, 1, 0)))
+        self.db = net.copy(lambda: (self.tmp.at[1], recv.at[1, 2:4], seq_dev(f, 3, 0)))
         self.c2 = {
             k: net.copy(lambda k=k: (acc.at[self.line(1, k)], recv2.at[k - 1], seq_dev(f, 0, k)))
             for k in ORDER
         }
 
+    def slots(self, k, at):
+        return self.src.at[pl.ds(self.line(0, k) * 4 + at, 2)]
+
     def line(self, axis, k):
         s = place()[0]
         x, y = s // 4, lax.rem(s, 4)
@@ -355,27 +362,54 @@
         )
 
     def near(self):
-        self.c1[1].start()
-        self.c1[3].start()
-
-    def far(self):
-        self.c1[2].start()
+        for c in (self.fa, self.fb, self.ub, self.da):
+            c.start()
+
+    def far(self, stage=None):
+        self.fa.wait_recv()
+        self.fb.wait_recv()
+        if stage is not None:
+            loads = [
+                pltpu.make_async_copy(a, b, self.sems.at[i])
+                for i, (a, b) in enumerate(
+                    (
+                        (self.slots(1, 0), self.tmp.at[0]),
+                        (self.slots(3, 2), self.tmp.at[1]),
+                        (self.recv.at[2, 0:2], stage[0].at[0:2]),
+                        (self.recv.at[2, 2:4], stage[1].at[0:2]),
+                    )
+                )
+            ]
+            for c in loads:
+                c.start()
+            for c in loads:
+                c.wait()
+        for e, c in ((0, self.ua), (1, self.db)):
+            for i in range(2):
+                if stage is None:
+                    own = self.src[self.line(0, 3 if e else 1) * 4 + 2 * e + i]
+                    way = self.recv[2, 2 * e + i]
+                else:
+                    own, way = self.tmp[e, i], stage[e][i]
+                self.tmp[e, i] = (own.astype(F32) + way.astype(F32)).astype(BF)
+            c.start()
 
     def p2(self, stage=None):
-        for k in ORDER:
-            self.c1[k].wait_recv()
+        for c in (self.ub, self.da, self.ua, self.db):
+            c.wait_recv()
         if stage is None:
             a = self.line(0, 0) * 4
 
             def body(j):
                 t = self.src[a + j].astype(F32) + self.recv[0, j].astype(F32)
-                t = t + self.recv[1, j].astype(F32) + self.recv[2, j].astype(F32)
-                self.acc[j] = t.astype(BF)
+                self.acc[j] = (t + self.recv[1, j].astype(F32)).astype(BF)
 
             fori(4, body)
         else:
             copies = [
-                pltpu.make_async_copy(self.recv.at[:, j], stage[j % 2], self.sems.at[j])
+                pltpu.make_async_copy(
+                    self.recv.at[0:2, j], stage[j % 2].at[0:2], self.sems.at[j]
+                )
                 for j in range(4)
             ]
             copies[0].start()
@@ -386,7 +420,7 @@
                 copies[j].wait()
                 st = stage[j % 2]
                 t = self.acc[j].astype(F32) + st[0].astype(F32)
-                self.acc[j] = (t + st[1].astype(F32) + st[2].astype(F32)).astype(BF)
+                self.acc[j] = (t + st[1].astype(F32)).astype(BF)
         for k in ORDER:
             self.c2[k].start()
 
@@ -570,11 +604,31 @@
         for i in range(4)
     ]
     tos = SeqGather(net, R.to, lambda q: cols128(R.toV, q), True, R.ls.at[4])
-    cks = SeqGather(net, R.ck, lambda q: rows128(R.ckF, q), True, R.ls.at[5])
-    cvs = SeqGather(net, R.cv, lambda q: cols128(R.cvF, q), False, R.ls.at[6])
-    crs = SeqGather(net, R.cr, lambda q: rows128(R.crF, q), False, R.ls.at[7])
-    sca = SeqScatter(net, R.gaH, R.ra1, R.ra2, R.ra3, True, R.ls.at[8], R.ls.at[20:24])
-    scb = SeqScatter(net, R.gbH, R.rb1, R.rb2, R.rb3, False, R.ls.at[9], R.ls.at[24:28])
+    cks = [
+        SeqGather(
+            net,
+            R.ck.at[:, a:e],
+            lambda q, a=a, e=e: R.ckF.at[pl.ds(pl.multiple_of(q * 128, 128), 128), a:e],
+            a == 0,
+            R.ls.at[5 + (a > 0)],
+        )
+        for a, e in ((0, 512), (512, FFL))
+    ]
+    cks.append(SeqGather(net, R.cr, lambda q: rows128(R.crF, q), False, R.ls.at[7]))
+    cvs = [
+        SeqGather(
+            net,
+            R.cv.at[a : a + FFL // 2],
+            lambda q, a=a: R.cvF.at[
+                a : a + FFL // 2, pl.ds(pl.multiple_of(q * 128, 128), 128)
+            ],
+            a == 0,
+            R.ls.at[36 + (a > 0)],
+        )
+        for a in (0, FFL // 2)
+    ]
+    sca = SeqScatter(net, R.gaH, R.ra1, R.ra2, R.ra3, None, True, R.ls.at[8], R.ls.at[20:24])
+    scb = SeqScatter(net, R.gbH, R.rb1, R.rb2, R.rb3, None, False, R.ls.at[9], R.ls.at[24:28])
 
     def seq_step(k):
         sq, hq = place()
@@ -799,7 +853,7 @@
             st = carry_wait(0, b, hmf)
             L.st[b] = st
             if b == 1:
-                for g in (cks, crs):
+                for g in cks:
                     g.p2(True)
 
             def body(c):
@@ -836,7 +890,7 @@
         shift(1)
         for t in tws:
             t.finish()
-        for g in (cks, crs, cvs):
+        for g in cks + cvs:
             g.p0()
         targets(0)
         states(0)
@@ -955,7 +1009,8 @@
 
             fori(4, square)
             if b == 0:
-                cvs.finish()
+                for g in cvs:
+                    g.finish()
                 loads[2].start()
                 loads[2].wait()
             rs1[b].drain()
@@ -1096,13 +1151,14 @@
 
         middle(0)
         rs1[1].pass_near()
-        for g in (cks, crs):
+        for g in cks:
             g.p3()
         midg[0].relay()
         midg[0].relay_far()
         middle(1)
-        cvs.p2(True)
-        for g in (cks, crs):
+        for g in cvs:
+            g.p2(True)
+        for g in cks:
             g.finish()
         for c in loads[0:2]:
             c.start()
@@ -1114,7 +1170,8 @@
         midg[1].relay_far()
         midg[1].finish()
         gkvg[0].relay()
-        cvs.p3()
+        for g in cvs:
+            g.p3()
         mixing(1)
         gkvg[0].relay_far()
         hidden_units(0)
@@ -1172,8 +1229,8 @@
 
     def time_backward(**kw):
         O = SimpleNamespace(**kw)
-        sea = SeqScatter(net, O.ea, R.ea1, O.ea2, R.ea3, True)
-        seb = SeqScatter(net, O.eb, R.eb1, O.eb2, R.eb3, False)
+        sea = SeqScatter(net, O.ea, R.ea1, O.ea2, R.ea3, O.eat, True)
+        seb = SeqScatter(net, O.eb, R.eb1, O.eb2, R.eb3, O.ebt, False)
         O.shT[...] = R.sh[...].T.astype(BF)
         for b in both:
             gkvg[b].drain()
@@ -1318,6 +1375,7 @@
 
                 return lax.fori_loop(0, 4, body, g8)
 
+            sca.tmp, scb.tmp = L.rat, L.rbt
             gzg[0].finish()
             gzg[1].relay()
             a10, a11 = gated(0)
@@ -1326,20 +1384,21 @@
             gzg[1].finish()
             b10, b11 = gated(1)
             adjoint(1)
-            sca.far()
-            scb.far()
+            scb.far([L.stage.at[0, :, 0:FFL], L.stage.at[1, :, 0:FFL]])
+            sca.far([L.stage.at[0], L.stage.at[1]])
             output_weight()
             seb.near()
-            seb.far()
             g9 = inner(0, z1)
             gate_weight()
             sea.near()
-            sea.far()
+            seb.far()
             g9 = inner(1, g9)
             scb.p2([L.stage.at[0, :, 0:FFL], L.stage.at[1, :, 0:FFL]])
+            sea.far()
             g8 = outer(0, z1)
             sca.p2([L.stage.at[0], L.stage.at[1]])
             g8 = outer(1, g8)
+            net.drain([sca.ua, sca.db, scb.ua, scb.db])
             R.gvec[0:1, :] = g8
             R.gvec[1:2, :] = g9
             R.gvec[2:3, :] = a10 + b10
@@ -1361,6 +1420,8 @@
             ds=pltpu.VMEM((2, W, W), F32),
             tsuf=pltpu.VMEM((16, W), F32),
             gatT=pltpu.VMEM((W, N), BF),
+            rat=pltpu.VMEM((2, 2, FFL + W, 128), BF),
+            rbt=pltpu.VMEM((2, 2, FFL, 128), BF),
             stage=pltpu.VMEM((2, 3, FFL + W, 128), BF),
         )
 
@@ -1375,8 +1436,8 @@
 
         def normed_back(**kw):
             L = SimpleNamespace(**kw)
-            sta = SeqScatter(net, L.ta, R.ta1, L.ta2, R.ta3, True)
-            stb = SeqScatter(net, L.tb, R.tb1, L.tb2, R.tb3, False)
+            sta = SeqScatter(net, L.ta, R.ta1, L.ta2, R.ta3, L.tat, True)
+            stb = SeqScatter(net, L.tb, R.tb1, L.tb2, R.tb3, L.tbt, False)
             sms = HeadScatter(net, L.sg, R.sgsib, L.sgsend, R.sgz)
             L.gsh[...] = jnp.zeros_like(L.gsh)
             rank = iota((160, W), 0)
@@ -1473,7 +1534,12 @@
                             axis=0,
                         ).astype(BF)
 
-                fori(8, body)
+                if b == 0:
+                    fori(8, body)
+                else:
+                    fori(4, body)
+                    rs4[0].pass_far()
+                    fori(4, lambda i: body(i + 4))
                 for k in (2, 1, 3, 0):
                     rs4[b].give(k)
 
@@ -1484,17 +1550,15 @@
             mixed_back(1)
             for c in last:
                 c.start()
+            for k in (2, 1, 3, 0):
+                sms.give(k)
             sta.far()
             stb.far()
-            rs4[0].pass_far()
-            for k in (2, 1, 3, 0):
-                sms.give(k)
+            rs4[0].pass_near()
+            sms.pass_far()
+            rs4[1].pass_far()
             sca.finish(R.oca)
             scb.finish(R.ocb)
-            rs4[0].pass_near()
-            rs4[1].pass_far()
-            sea.finish(R.oea)
-            seb.finish(R.oeb)
             for c in last:
                 c.wait_recv()
             edge = jnp.sum(R.brecv[...], axis=0)
@@ -1511,15 +1575,8 @@
             R.rrecv[h] = R.rsend[...]
             for c in rex:
                 c.start()
+            sms.pass_near()
             rs4[1].pass_near()
-            sms.pass_far()
-            sta.p2()
-            stb.p2()
-            for c in rex:
-                c.wait_recv()
-            tot = jnp.sum(R.rrecv[...], axis=0)
-            L.rsum[...] = jnp.concatenate([tot, jnp.zeros((120, N), F32)], axis=0).T / D
-            sms.pass_near()
             g0, g1 = z1, z1
             for b in both:
                 rows = rows_of(b)
@@ -1529,17 +1586,33 @@
                 n = (R.xF[b, h].astype(F32) - R.mean[rows, :]) * R.rstd[rows, :]
                 g0 = g0 + jnp.sum(gl * n, axis=0, keepdims=True)
                 g1 = g1 + jnp.sum(gl, axis=0, keepdims=True)
+            O.lsm[0:400, :] = sms.total()
+            O.lsm[R_VEC : R_VEC + 2, :] += jnp.concatenate([g0, g1], axis=0)
+            O.lsm[R_VEC + 8 : R_VEC + 12, :] += R.gvec[0:4, :]
+            packed = lax.dot_general(
+                R.sel[...],
+                O.lsm[...].astype(BF),
+                (((0,), (0,)), ((), ())),
+                preferred_element_type=F32,
+            )
+            R.psend[...] = packed.astype(BF).reshape(16, 32, W)
+            for c in smo:
+                c.start()
+            sta.p2()
+            stb.p2()
+            for c in rex:
+                c.wait_recv()
+            tot = jnp.sum(R.rrecv[...], axis=0)
+            L.rsum[...] = jnp.concatenate([tot, jnp.zeros((120, N), F32)], axis=0).T / D
+            for b in both:
+                rows = rows_of(b)
+                gl = R.mid[b].reshape(TB, W)
+                n = (R.xF[b, h].astype(F32) - R.mean[rows, :]) * R.rstd[rows, :]
                 R.hgrad[b] = slab_of(R.midF.at[b], h).astype(F32) + R.rstd[rows, :] * (
                     gl * vl[0:1] - L.rsum[rows, 0:1] - n * L.rsum[rows, 1:2]
                 )
-            O.lsm[0:400, :] = sms.total()
-            O.lsm[R_VEC : R_VEC + 2, :] += jnp.concatenate([g0, g1], axis=0)
-            O.lsm[R_VEC + 8 : R_VEC + 12, :] += R.gvec[0:4, :]
-            R.psend[...] = (
-                lax.dot_general(R.sel[...], O.lsm[...].astype(BF), (((0,), (0,)), ((), ())), preferred_element_type=F32).astype(BF).reshape(16, 32, W)
-            )
-            for c in smo:
-                c.start()
+            sea.finish(R.oea)
+            seb.finish(R.oeb)
             R.psrecv[s] = R.psend[s]
             for c in smo:
                 c.wait_recv()
@@ -1555,6 +1628,8 @@
             ta=pltpu.VMEM((16, RT, 128), BF),
             tb=pltpu.VMEM((16, RT, 128), BF),
             ta2=pltpu.VMEM((4, RT, 128), BF),
+            tat=pltpu.VMEM((2, 2, RT, 128), BF),
+            tbt=pltpu.VMEM((2, 2, RT, 128), BF),
             tb2=pltpu.VMEM((4, RT, 128), BF),
             sg=pltpu.VMEM((8, 400, W), BF),
             sgsend=pltpu.VMEM((3, 400, W), BF),
@@ -1570,10 +1645,12 @@
         ea=pltpu.VMEM((16, W, 128), BF),
         eb=pltpu.VMEM((16, W, 128), BF),
         ea2=pltpu.VMEM((4, W, 128), BF),
+        eat=pltpu.VMEM((2, 2, W, 128), BF),
+        ebt=pltpu.VMEM((2, 2, W, 128), BF),
         eb2=pltpu.VMEM((4, W, 128), BF),
-        shT=pltpu.VMEM((160, N), BF),
         gp=pltpu.VMEM((4, N, W), BF),
         gpT=pltpu.VMEM((4, W, N), BF),
+        shT=pltpu.VMEM((160, N), BF),
         gw=pltpu.VMEM((N, W), BF),
         gdp=pltpu.VMEM((N, 64), BF),
         gdpT=pltpu.VMEM((64, N), BF),
@@ -1690,7 +1767,7 @@
         tb1=((3, 4, RT, 128), BF),
         tb3=((3, RT, 128), BF),
     )
-    sems = dict(ss=430, rs=430, ls=36, bs=18, br=18, cs=64, cr_=64)
+    sems = dict(ss=480, rs=480, ls=38, bs=18, br=18, cs=64, cr_=64)
     names = list(ins) + list(outs) + list(scr) + list(sems)
     got = pl.pallas_call(
         functools.partial(layer_kernel, names),

time: 318 us -> 300 us (0.943)
  Pallas kernels: 312 us -> 295 us
    pallas_call x1, Pallas kernels: 309 us -> 291 us  [run_layer(): pl.pallas_call(functools.partial(layer_kernel, names), out_shape=[SD(a, t...]
where the time goes in v1:
time: 300 us
  Pallas kernels  295 us (98%)
  local copies, waits for them, and re-layouts  3.52 us (1%)
    pallas_call x1, Pallas kernels, run_layer(): pl.pallas_call(functools.partial(layer_kernel, names), out_shape=[SD(a, t...  291 us

profile of v1, /device:TPU:1, one launch (start us, length us, event | category | flops | bytes accessed | tf_op | source)
XLA Modules:
  0.0 299.8 jit_solution(22453871970923290)
XLA Ops:
  0.6 0.7 subtract_bitcast_fusion
  1.3 0.9 copy.36
  2.2 291.5 %layer.1 = (f32[2,256,256]{2,1,0:T(8,128)}, f32[2,256,256]{2,1,0:T(8,128)}, f32[1152,128]{1,0:T(8,128)}, f32[896,128]{1,0:T(8,128)}, f32[256,128]{1,0:T(8,128)},...) custom-call(bf16[2,256,256]{2,1,0:T(8,128)(2,1)} %refs_0_.1, ...), custom_call_target="tpu_custom_call" | custom-call | tf_op jit(solution)/shard_map/layer/pallas_call | solution.py:1772
  293.7 3.5 %finish.1 = (f32[2,256,256]{2,1,0:T(8,128)}, f32[2,256,256]{2,1,0:T(8,128)}, f32[1,1,256]{2,1,0:T(1,128)}, f32[1,10,256]{2,1,0:T(8,128)}, f32[1,10,256]{2,1,0:T(...) custom-call(f32[2,256,256]{2,1,0:T(8,128)} %get-tuple-element.21.res, ...), custom_call_target="tpu_custom_call" | custom-call | tf_op jit(solution)/shard_map/finish/pallas_call | solution.py:1845
  297.2 1.3 copy.33
  298.5 1.3 copy.34
  (1 shorter events, 0.0 us)

commit v2 on v1

--- a/solution.py
+++ b/solution.py
@@ -1821,8 +1821,8 @@
 ):
     o_result[...] = result[...]
     o_hidden[...] = hg[...]
-    o_first[0] = sm[0:10]
-    o_second[0] = sm[10:20]
+    o_first[...] = sm[0:10].reshape(10, 1, W)
+    o_second[...] = sm[10:20].reshape(10, 1, W)
     o_decay1[0] = sm[20:24]
     o_decay2[0] = sm[24:28]
     o_vec[0] = sm[28:29]
@@ -1839,10 +1839,10 @@
 
 def finish(*ins):
     shapes = [
-        (2, TB, W), (2, TB, W), (1, 1, W), (1, 10, W), (1, 10, W), (1, 4, W), (1, 4, W),
+        (2, TB, W), (2, TB, W), (1, 1, W), (10, 1, W), (10, 1, W), (1, 4, W), (1, 4, W),
         (1, 4, 128, W), (1, W, 128), (1, 128, FFL), (1, FFL, 128), (1, 128, W),
     ]
-    return pl.pallas_call(
+    got = pl.pallas_call(
         finish_kernel,
         out_shape=[SD(q, F32) for q in shapes],
         in_specs=[VM] * len(ins),
@@ -1850,6 +1850,7 @@
         name="finish",
         compiler_params=pltpu.CompilerParams(vmem_limit_bytes=VMEM_LIMIT),
     )(*ins)
+    return tuple(a.transpose(1, 0, 2) if a.shape[:2] == (10, 1) else a for a in got)
 
 
 def solution(mesh):

time: 300 us -> 298 us (level)
  no operation moved by 1% of the time
where the time goes in v2:
time: 298 us; the launch traced here: 297 us
  Pallas kernels  295 us (99%)
    pallas_call x1, Pallas kernels, run_layer(): pl.pallas_call(functools.partial(layer_kernel, names), out_shape=[SD(a, t...  291 us

profile of v2, /device:TPU:1, one launch (start us, length us, event | category | flops | bytes accessed | tf_op | source)
XLA Modules:
  0.0 297.3 jit_solution(3484211632851424303)
XLA Ops:
  0.6 0.7 subtract_bitcast_fusion
  1.3 0.9 copy.32
  2.2 291.5 %layer.1 = (f32[2,256,256]{2,1,0:T(8,128)}, f32[2,256,256]{2,1,0:T(8,128)}, f32[1152,128]{1,0:T(8,128)}, f32[896,128]{1,0:T(8,128)}, f32[256,128]{1,0:T(8,128)},...) custom-call(bf16[2,256,256]{2,1,0:T(8,128)(2,1)} %refs_0_.1, ...), custom_call_target="tpu_custom_call" | custom-call | tf_op jit(solution)/shard_map/layer/pallas_call | solution.py:1772
  293.7 3.6 %finish.1 = (f32[2,256,256]{2,1,0:T(8,128)}, f32[2,256,256]{2,1,0:T(8,128)}, f32[1,1,256]{2,1,0:T(1,128)}, f32[10,1,256]{2,1,0:T(1,128)}, f32[10,1,256]{2,1,0:T(...) custom-call(f32[2,256,256]{2,1,0:T(8,128)} %get-tuple-element.33.res, ...), custom_call_target="tpu_custom_call" | custom-call | tf_op jit(solution)/shard_map/finish/pallas_call | solution.py:1845
  (1 shorter events, 0.0 us)
